TPU v7x, 512 devices: a whole 4x4x16 slice. The times are simulated.
512 devices in a mesh: dp: 32 (over y_hi, z), owner: 16 (over y_lo, x, core).
Axes of the slice: x: 4, y: 4 (y_hi: 2, y_lo: 2; y = y_hi * 2 + y_lo), z: 16, core: 2. Of those that a mesh axis runs over, the one named last changes fastest.
Arguments:
- gate_pre: bfloat16 [12288, 16, 6, 128], P('dp', 'owner'), may hold values from -6 to 6
- up_pre: bfloat16 [12288, 16, 6, 128], P('dp', 'owner'), may hold values from -6 to 6
- out_grad: bfloat16 [12288, 2560], P('dp'), may hold values from -6 to 6
- down_weight: bfloat16 [16, 2560, 6, 128], P('owner', 'dp'), may hold values from -0.125 to 0.125
- old_first: float32 [16, 2560, 9, 128], P('owner', 'dp'), may hold values from -8 to 8
- old_second: float32 [16, 2560, 9, 128], P('owner', 'dp'), may hold values from 0.5 to 16
- old_owner: int32 [54], replicated, may hold values from 0 to 7, as said below
- new_owner: int32 [54], replicated, may hold values from 0 to 15, as said below
Outputs:
- d_gate: bfloat16 [12288, 16, 6, 128], P('dp', 'owner')
- d_up: bfloat16 [12288, 16, 6, 128], P('dp', 'owner')
- new_first: float32 [16, 2560, 6, 128], P('owner', 'dp')
- new_second: float32 [16, 2560, 6, 128], P('owner', 'dp')
- step_dir: float32 [16, 2560, 6, 128], P('owner', 'dp')
Inputs may be any that keep to these rules, and one draw needn't show every extreme that they name: `old_owner`: only owners 0 to 7 hold slabs; each holds at most 9 slabs and one holds exactly 9. `new_owner`: each owner holds at most 6 slabs and one holds exactly 6.
All inputs are finite; a program needn't handle non-finite values.
Results may differ from a plain program's by a relative error of at most 0.0075.
Values may be sent and summed in bfloat16 or wider, within the bound.
A program may use at most 128 MiB of HBM per device.

v0:
```python
import jax
import jax.numpy as jnp
from jax import lax
from jax.sharding import PartitionSpec as P


def slot_ranks(owner_map, groups):
    onehot = (owner_map[:, None] == jnp.arange(groups, dtype=jnp.int32)[None, :]).astype(jnp.int32)
    before = jnp.cumsum(onehot, axis=0) - onehot
    return (jnp.sum(before * onehot, axis=1), jnp.sum(onehot, axis=0))


def per_device(
    gate_pre, up_pre, out_grad, down_weight, old_first, old_second, old_owner, new_owner
):
    groups = lax.axis_size("owner")
    own_index = lax.axis_index("owner")
    replicas = lax.axis_size("dp")
    tokens_dev = out_grad.shape[0]
    capacity = gate_pre.shape[2]
    slab_width = gate_pre.shape[3]
    old_capacity = old_first.shape[2]
    width_rows = old_first.shape[1]
    new_rank, new_count = slot_ranks(new_owner, groups)
    old_rank, old_count = slot_ranks(old_owner, groups)
    held = jnp.sum(jnp.where(jnp.arange(groups, dtype=jnp.int32) == own_index, new_count, 0))
    live_slots = (jnp.arange(capacity, dtype=jnp.int32) < held).astype(jnp.float32)
    gate32 = gate_pre[:, 0].astype(jnp.float32)
    up32 = up_pre[:, 0].astype(jnp.float32)
    sigmoid_gate = jax.nn.sigmoid(gate32)
    hidden = (
        (gate32 * sigmoid_gate * up32)
        .astype(jnp.bfloat16)
        .reshape(tokens_dev, capacity * slab_width)
    )
    piece = lax.all_gather(down_weight, "dp", axis=1, tiled=True)
    rows = piece.shape[1]
    block = out_grad
    hidden_grad = jnp.dot(
        block, piece.reshape(rows, capacity * slab_width), preferred_element_type=jnp.float32
    )
    hidden_grad = hidden_grad.reshape(tokens_dev, capacity, slab_width) * live_slots[None, :, None]
    d_gate = (hidden_grad * up32 * sigmoid_gate * (1.0 + gate32 * (1.0 - sigmoid_gate))).astype(
        jnp.bfloat16
    )[:, None]
    d_up = (hidden_grad * gate32 * sigmoid_gate).astype(jnp.bfloat16)[:, None]
    block = out_grad
    grad_rows = lax.psum_scatter(
        lax.dot_general(
            block, hidden, (((0,), (0,)), ((), ())), preferred_element_type=jnp.float32
        ).astype(jnp.bfloat16),
        "dp",
        scatter_dimension=0,
        tiled=True,
    ).astype(jnp.float32)
    gradient = grad_rows.reshape(width_rows, capacity, slab_width) * (tokens_dev * replicas) ** (
        -0.5
    )
    mine = (
        (new_owner[None, :] == own_index)
        & (new_rank[None, :] == jnp.arange(capacity, dtype=jnp.int32)[:, None])
    ).astype(jnp.float32)
    old_slots = (old_rank[None, :] == jnp.arange(old_capacity, dtype=jnp.int32)[:, None]).astype(
        jnp.float32
    )
    zeros_state = jnp.zeros((width_rows, capacity, slab_width), jnp.float32)
    pieces = (
        lax.all_gather(old_first.astype(jnp.bfloat16), "owner", axis=0, tiled=True).astype(
            jnp.float32
        ),
        lax.all_gather(old_second.astype(jnp.bfloat16), "owner", axis=0, tiled=True).astype(
            jnp.float32
        ),
    )
    count = pieces[0].shape[0]
    sources = jnp.arange(count, dtype=jnp.int32)
    from_source = (old_owner[None, :] == sources[:, None]).astype(jnp.float32)
    select = jnp.einsum(
        "qs,js,ks->qjk", from_source, old_slots, mine, precision=lax.Precision.HIGHEST
    )
    first_add = jnp.einsum("qdjs,qjk->dks", pieces[0], select, precision=lax.Precision.HIGHEST)
    second_add = jnp.einsum("qdjs,qjk->dks", pieces[1], select, precision=lax.Precision.HIGHEST)
    prior_first = zeros_state + first_add
    prior_second = zeros_state + second_add
    mask = live_slots[None, :, None]
    first = 0.9 * prior_first + 0.1 * gradient
    second = 0.95 * prior_second + 0.05 * gradient * gradient
    step_dir = first / (1.0 - 0.9**20) / (jnp.sqrt(second / (1.0 - 0.95**20)) + 1e-08)
    return (d_gate, d_up, (first * mask)[None], (second * mask)[None], (step_dir * mask)[None])


def solution(mesh):
    return jax.shard_map(
        per_device,
        mesh=mesh,
        in_specs=(
            P("dp", "owner", None, None),
            P("dp", "owner", None, None),
            P("dp", None),
            P("owner", "dp", None, None),
            P("owner", "dp", None, None),
            P("owner", "dp", None, None),
            P(),
            P(),
        ),
        out_specs=(
            P("dp", "owner", None, None),
            P("dp", "owner", None, None),
            P("owner", "dp", None, None),
            P("owner", "dp", None, None),
            P("owner", "dp", None, None),
        ),
        check_vma=False,
    )
```

profile of v0, /device:TPU:24, one launch (start us, length us, event | category | flops | bytes accessed | tf_op | source)
XLA Modules:
  0.0 962.9 jit_solution(17343598262908662232)
XLA Ops:
  7.2 0.0 copy-start
  7.2 0.0 all-gather.4.cloned.1.call-start
  7.2 0.7 all-gather.4.cloned.1.call-update
  7.9 0.0 reduce-scatter.4.cloned.1.call-start
  8.0 1.3 copy.49
  9.3 2.3 copy.50
  11.6 1.6 fusion.19
  13.2 0.0 copy-done
  13.2 4.2 fusion
  17.4 6.3 copy.59
  23.7 0.0 copy-start.3
  23.7 0.0 copy-start.4
  23.7 0.0 reduce-scatter.4.cloned.1.call-update
  23.7 0.0 copy-start.6
  23.7 0.0 copy-start.5
  23.8 0.0 all-gather.8.cloned.1.call-start
  23.8 0.9 copy-done.3
  24.7 0.7 convert_element_type.85
  25.4 0.0 all-gather.8.cloned.1.call-update
  25.4 0.0 all-gather.6.cloned.1.call-start
  25.5 0.0 copy-done.4
  25.5 0.7 convert_element_type.76
  26.2 0.0 all-gather.6.cloned.1.call-update
  26.2 0.0 copy-done.6
  26.2 0.1 fusion.58
  26.3 0.1 reduce_window_sum.17
  26.4 0.0 copy-done.5
  26.4 0.1 fusion.57
  26.4 0.1 reduce_window_sum.18
  26.5 0.2 select_reduce_fusion.1
  26.7 0.6 fusion.68
  27.4 0.6 compare_convert_fusion
  28.0 0.2 select_reduce_fusion
  28.2 0.2 convolution_bitcast_fusion
  28.4 0.0 copy-start.1
  28.4 0.0 copy-start.2
  28.4 147.7 %all-gather.4.cloned.1.call-done = bf16[1,2560,6,128]{3,1,2,0:T(8,128)(2,1)} async-done(((bf16[1,80,6,128]{3,1,2,0:T(8,128)(2,1)}), bf16[1,2560,6,128]{3,1,2,0:T(8,128)(2,1)}) %all-gather.4.cloned.1.call-update) | async-done | bytes 3932176 | tf_op jit(solution)/shard_map/all_gather | solution.py:36
  176.1 6.4 copy.46
  182.5 0.0 copy-done.1
  182.5 0.0 copy-done.2
  182.5 5.2 fusion.50
  187.7 673.1 %reduce-scatter.4.cloned.1.call-done = bf16[80,768]{1,0:T(8,128)(2,1)} async-done(((bf16[2560,768]{1,0:T(8,128)(2,1)}), bf16[80,768]{1,0:T(8,128)(2,1)}) %reduce-scatter.4.cloned.1.call-update) | async-done | bytes 122896 | tf_op jit(solution)/shard_map/reduce_scatter | solution.py:48
  860.8 0.9 fusion.52
  861.9 42.9 %all-gather.8.cloned.1.call-done = bf16[16,80,9,128]{3,1,2,0:T(8,128)(2,1)} async-done(((bf16[1,80,9,128]{3,1,2,0:T(8,128)(2,1)}), bf16[16,80,9,128]{3,1,2,0:T(8,128)(2,1)}) %all-gather.8.cloned.1.call-update) | async-done | bytes 2949136 | tf_op jit(solution)/shard_map/all_gather | solution.py:71
  904.8 3.3 fusion.38
  908.1 42.7 %all-gather.6.cloned.1.call-done = bf16[16,80,9,128]{3,1,2,0:T(8,128)(2,1)} async-done(((bf16[1,80,9,128]{3,1,2,0:T(8,128)(2,1)}), bf16[16,80,9,128]{3,1,2,0:T(8,128)(2,1)}) %all-gather.6.cloned.1.call-update) | async-done | bytes 2949136 | tf_op jit(solution)/shard_map/all_gather | solution.py:68
  950.8 3.3 multiply_bitcast_fusion
  954.1 0.7 copy.54
  954.8 0.7 copy.55
  955.6 0.7 copy.56
  (5 shorter events, 0.1 us)
Async XLA Ops:
  7.2 6.0 copy-start
  7.2 169.0 %all-gather.4.cloned.1.call-start = ((), (), s32[]{:S(2)}) async-start(), calls=%async_computation.1 | async-start | bytes 4055040 | tf_op jit(solution)/shard_map/all_gather | solution.py:36
  7.9 852.9 %reduce-scatter.4.cloned.1.call-start = ((), (), s32[]{:S(2)}) async-start(), calls=%async_computation.4 | async-start | bytes 4055040 | tf_op jit(solution)/shard_map/reduce_scatter | solution.py:48
  23.7 1.0 copy-start.3
  23.7 1.8 copy-start.4
  23.7 2.5 copy-start.6
  23.7 2.6 copy-start.5
  23.8 881.0 %all-gather.8.cloned.1.call-start = ((), (), s32[]{:S(2)}) async-start(), calls=%async_computation.3 | async-start | bytes 3133440 | tf_op jit(solution)/shard_map/all_gather | solution.py:71
  25.4 925.4 %all-gather.6.cloned.1.call-start = ((), (), s32[]{:S(2)}) async-start(), calls=%async_computation.2 | async-start | bytes 3133440 | tf_op jit(solution)/shard_map/all_gather | solution.py:68
  28.4 154.1 %copy-start.1 = (bf16[384,1,6,128]{3,0,2,1:T(8,128)(2,1)S(1)}, bf16[384,1,6,128]{3,0,2,1:T(8,128)(2,1)}, u32[]{:S(2)}) copy-start(bf16[384,1,6,128]{3,0,2,1:T(8,128)(2,1)} %param.8) | copy-start | bytes 1769476
  28.4 154.1 %copy-start.2 = (bf16[384,1,6,128]{3,0,2,1:T(8,128)(2,1)S(1)}, bf16[384,1,6,128]{3,0,2,1:T(8,128)(2,1)}, u32[]{:S(2)}) copy-start(bf16[384,1,6,128]{3,0,2,1:T(8,128)(2,1)} %param.9) | copy-start | bytes 1769476
Sparse Core Ops, SparseCore 0:
  11.0 165.1 all-gather.3
  180.6 680.1 reduce-scatter.3
  863.5 41.1 all-gather.7
  907.3 43.3 all-gather.5
where the time goes:
time: 965 us; the launch traced here: 963 us
  waiting for transfers between devices  907 us (94%)
  local copies, waits for them, and re-layouts  19.5 us (2%)
  matrix products  16.1 us (2%)
  between operations  13.9 us (1%)
    reduce_scatter x1, waiting for transfers between devices, per_device(): lax.psum_scatter(lax.dot_general(block, hidden, (((0,), (0,)), ((), ())),...  673 us
    all_gather x1, waiting for transfers between devices, per_device(): piece = lax.all_gather(down_weight, 'dp', axis=1, tiled=True)  148 us
    all_gather x1, waiting for transfers between devices, per_device(): lax.all_gather(old_second.astype(jnp.bfloat16), 'owner', axis=0, tiled=True)  42.9 us
    all_gather x1, waiting for transfers between devices, per_device(): lax.all_gather(old_first.astype(jnp.bfloat16), 'owner', axis=0, tiled=True)  42.7 us
  transfers between devices with their start and end apart: 4, of which 4 were waited for; matrix products, arithmetic and copies ran while one was open for 4% of the time, Pallas kernels for 0%

commit v1 on v0

v1 whole, which is shorter than its diff:
```python
import functools

import jax
import jax.numpy as jnp
from jax import lax
from jax.experimental import pallas as pl
from jax.experimental.pallas import tpu as pltpu
from jax.sharding import PartitionSpec as P

MESH = pl.DeviceIdType.MESH
BF, F32 = jnp.bfloat16, jnp.float32
NZ, NY, NX = 16, 4, 4
HOPS = 8
CAP, CAP_OLD, SLAB = 6, 9, 128
TOK, WIDTH = 384, 2560
HALF = WIDTH // 2
ROWS = WIDTH // 32
COLS = CAP * SLAB
SUB = COLS // 2
UNIT = TOK // 8
GB = 256
N_SLAB = 54
LR1, LR2 = 0.9, 0.95

SEM = {}


def _number(*names):
    for n in names:
        SEM[n] = len(SEM)


for _s in range(HOPS):
    for _d in range(2):
        for _k in range(2):
            _number(("ag", _d, _s, _k), ("rs", _d, _s, _k))
_number(("og",), ("ogx", 0), ("ogx", 1), ("ogx", 2), *[("ogc", i) for i in range(4)])
for _r in range(2):
    for _d in range(2):
        _number(("hid", _d, _r), ("hg", _d, _r))
for _i in range(2):
    _number(("my", _i), ("mx", 0, _i), ("mx", 1, _i), ("mf", _i))
    _number(*[("mc", j, _i) for j in range(4)])


def body(
    gate, up, og, w, m1, m2, old_map, new_map,
    dg_out, du_out, nf_out, ns_out, sd_out,
    gate_v, up_v, fg, fu, m1_v, m2_v, og_v, hid, hgs, hgr, hg_own,
    wb, gb, rsb, mb, grad, dg_v, du_v, nf_v, ns_v, sd_v,
    ssem, rsem, lsem,
):
    dp, ow = lax.axis_index("dp"), lax.axis_index("owner")
    hi, z = dp // NZ, dp % NZ
    lo, x, core = ow // 8, (ow // 2) % NX, ow % 2
    y = hi * 2 + lo

    def dev(y_, x_, z_, c_):
        return ((y_ // 2) * NZ + z_, (y_ % 2) * 8 + x_ * 2 + c_)

    zn = (dev(y, x, (z + 1) % NZ, core), dev(y, x, (z + NZ - 1) % NZ, core))
    far = dev((y + 2) % NY, x, z, core)
    lows = dev((y // 2) * 2 + 1 - lo, x, z, core)
    xn = (dev(y, (x + 1) % NX, z, core), dev(y, (x + NX - 1) % NX, z, core))
    cn = dev(y, x, z, 1 - core)
    other = dev((y + NY - 1 + 2 * lo) % NY, x, z, core)

    started = []

    def copy(name, src, dst, device):
        i = SEM[name]
        return pltpu.make_async_remote_copy(
            src_ref=src, dst_ref=dst, send_sem=ssem.at[i], recv_sem=rsem.at[i],
            device_id=device, device_id_type=MESH,
        )

    def send(name, src, dst, device):
        c = copy(name, src, dst, device)
        c.start()
        started.append(c)

    def arrived(name, dst, device):
        copy(name, dst, dst, device).wait_recv()

    def local(i, src, dst):
        return pltpu.make_async_copy(src, dst, lsem.at[i])

    def rows_of(t):
        return pl.ds(pl.multiple_of(t * ROWS, 16), ROWS)

    def sub(k):
        return pl.ds(k * SUB, SUB)

    mine_d = pl.ds(pl.multiple_of(hi * HALF, 128), HALF)
    other_d = pl.ds(pl.multiple_of((1 - hi) * HALF, 128), HALF)

    loads_w = [local(i, w.at[i], wb.at[rows_of(z), pl.ds(i * SLAB, SLAB)]) for i in range(CAP)]
    load_gate, load_up = local(6, gate, gate_v), local(7, up, up_v)
    load_og = local(8, og.at[:, mine_d], og_v.at[pl.ds(0, TOK)])
    load_m = [local(9, m1, m1_v), local(10, m2, m2_v)]
    for c in [*loads_w, load_gate, load_up, load_og, *load_m]:
        c.start()

    barrier = pltpu.get_barrier_semaphore()
    for n in (*zn, *xn, cn, far, other, lows):
        pl.semaphore_signal(barrier, inc=1, device_id=n, device_id_type=MESH)
    pl.semaphore_wait(barrier, 8)

    def unit(x_, c_):
        return pl.ds(pl.multiple_of((x_ * 2 + c_) * UNIT, 16), UNIT)

    def og_part(x_, c_):
        return og_v.at[pl.ds(pl.multiple_of(TOK + (x_ * 2 + c_) * UNIT, 16), UNIT)]

    send(("og",), og.at[unit(x, core), other_d], og_part(x, core), other)

    def hops(d, k):
        return HOPS if d == k else HOPS - 1

    def ag_slot(d, s):
        return (z + NZ - s) % NZ if d == 0 else (z + s) % NZ

    def ag_tick(s):
        for k in range(2):
            for d in range(2):
                if 0 < s <= hops(d, k):
                    dst = wb.at[rows_of(ag_slot(d, s)), sub(k)]
                    arrived(("ag", d, s - 1, k), dst, zn[d])
                if s < hops(d, k):
                    ref = wb.at[rows_of(ag_slot(d, s)), sub(k)]
                    send(("ag", d, s, k), ref, ref, zn[d])

    def rs_dest(d, s, k):
        n = hops(d, k)
        return (z + n - s) % NZ if d == 0 else (z + NZ - n + s) % NZ

    def rs_tick(s):
        for k in range(2):
            for d in range(2):
                if s >= hops(d, k):
                    continue
                mine = gb.at[rows_of(rs_dest(d, s, k)), sub(k)]
                if s == 0:
                    src = mine
                else:
                    src = rsb.at[d, s - 1, :, sub(k)]
                    arrived(("rs", d, s - 1, k), src, zn[d])
                    src[...] = (src[...].astype(F32) + mine[...].astype(F32)).astype(BF)
                send(("rs", d, s, k), src, rsb.at[d, s, :, sub(k)], zn[d])

    for c in loads_w:
        c.wait()
    ag_tick(0)

    load_gate.wait()
    load_up.wait()
    step = 64

    def hidden_rows(first):
        for slot in range(CAP):

            @pl.loop(0, TOK // 2 // step)
            def _(i):
                r = pl.ds(pl.multiple_of(first + i * step, step), step)
                g = gate_v[slot, r, :].astype(F32)
                u = up_v[slot, r, :].astype(F32)
                sig = jax.nn.sigmoid(g)
                gs = g * sig
                hid[r, pl.ds(slot * SLAB, SLAB)] = (gs * u).astype(BF)
                fu[slot, r, :] = gs
                fg[slot, r, :] = u * sig * (1.0 + g * (1.0 - sig))

    def half(r):
        return pl.ds(r * (TOK // 2), TOK // 2)

    def partner(r):
        return pl.ds(TOK + r * (TOK // 2), TOK // 2)

    for r in range(2):
        hidden_rows(r * (TOK // 2))
        for d in range(2):
            send(("hid", d, r), hid.at[half(r), sub(d)], hid.at[partner(r), sub(d)], far)

    me = x * 2 + core

    for c in load_m:
        c.wait()

    def to_y(i):
        ref = mb.at[me, i]
        return copy(("my", i), ref, ref, lows)

    @pl.when(lo == 0)
    def _():
        @pl.loop(0, CAP_OLD)
        def _(j):
            mb[me, 0, j] = m1_v[j].astype(BF)
            mb[me, 1, j] = m2_v[j].astype(BF)

        for i in range(2):
            to_y(i).start()

    ag_tick(1)

    def og_to(name, x_, device):
        send(name, og_part(x_, core), og_part(x_, core), device)

    x1, x2, x3 = (x + 1) % NX, (x + 2) % NX, (x + 3) % NX
    arrived(("og",), og_part(x, core), other)
    og_to(("ogx", 0), x, xn[0])
    og_to(("ogx", 1), x, xn[1])
    og_to(("ogc", 0), x, cn)

    ag_tick(2)

    arrived(("ogx", 0), og_part(x3, core), xn[0])
    og_to(("ogx", 2), x3, xn[0])
    og_to(("ogc", 1), x3, cn)
    arrived(("ogx", 1), og_part(x1, core), xn[1])
    og_to(("ogc", 2), x1, cn)

    ag_tick(3)

    @pl.when(lo == 1)
    def _():
        for i in range(2):
            to_y(i).wait_recv()

    def mom(x_, i):
        return mb.at[x_ * 2 + core, i]

    def mom_to(name, x_, i, device):
        send(name, mom(x_, i), mom(x_, i), device)

    for i in range(2):
        for d in range(2):
            mom_to(("mx", d, i), x, i, xn[d])
        mom_to(("mc", 0, i), x, i, cn)

    ag_tick(4)
    arrived(("ogx", 2), og_part(x2, core), xn[0])
    og_to(("ogc", 3), x2, cn)
    ag_tick(5)
    for i, x_ in enumerate((x, x3, x1, x2)):
        arrived(("ogc", i), og_part(x_, 1 - core), cn)
    load_og.wait()
    for r in range(2):
        for d in range(2):
            arrived(("hid", d, r), hid.at[partner(r), sub(d)], far)

    def grad_block(i):
        part = lax.dot_general(
            og_v[:, pl.ds(i * GB, GB)], hid[...], (((0,), (0,)), ((), ())),
            preferred_element_type=F32,
        )
        gb[pl.ds(i * GB, GB), :] = part.astype(BF)

    grad_block(0)
    ag_tick(6)
    grad_block(1)
    grad_block(2)
    ag_tick(7)
    grad_block(3)
    grad_block(4)
    rs_tick(0)
    ag_tick(8)

    for d, x_ in enumerate((x3, x1)):
        for i in range(2):
            arrived(("mx", d, i), mom(x_, i), xn[d])
        mom_to(("mf", d), x_, d, xn[d])
        for i in range(2):
            mom_to(("mc", 1 + d, i), x_, i, cn)

    def hidden_grad(first, out):
        @pl.loop(0, 3)
        def _(j):
            cols = pl.ds(pl.multiple_of(j * 256, 256), 256)
            out[:, cols] = jnp.dot(
                og_v[pl.ds(first, TOK), :], wb[:, cols], preferred_element_type=F32
            ).astype(out.dtype)

    hidden_grad(TOK, hgs)
    for r in range(2):
        for d in range(2):
            send(("hg", d, r), hgs.at[half(r), sub(d)], hgr.at[half(r), sub(d)], far)
    rs_tick(1)
    hidden_grad(0, hg_own)

    same = (N_SLAB, N_SLAB)
    lane, row = lax.broadcasted_iota(jnp.int32, same, 1), lax.broadcasted_iota(jnp.int32, same, 0)
    diagonal, earlier = lane == row, row < lane

    def owners_ranks(ref):
        across = jnp.broadcast_to(ref[...], same)
        down = jnp.sum(jnp.where(diagonal, across, 0), axis=1, keepdims=True)
        rank = jnp.sum(jnp.where((across == down) & earlier, 1, 0), axis=0, keepdims=True)
        return ref[...], rank

    old_own, old_rank = owners_ranks(old_map)
    new_own, new_rank = owners_ranks(new_map)
    slots = []
    for k in range(CAP):
        here = (new_own == ow) & (new_rank == k)
        slots.append(
            tuple(jnp.sum(jnp.where(here, v, 0)) for v in (old_own, old_rank, jnp.ones_like(old_own)))
        )

    rs_tick(2)

    rs_tick(3)
    for d in range(2):
        arrived(("mf", d), mom(x2, d), xn[d])
        mom_to(("mc", 3, d), x2, d, cn)
    rs_tick(4)
    rs_tick(5)
    rs_tick(6)

    for r in range(2):
        for d in range(2):
            arrived(("hg", d, r), hgr.at[half(r), sub(d)], far)
    for k in range(CAP):
        live = slots[k][2].astype(F32)

        @pl.loop(0, TOK // step)
        def _(i):
            r = pl.ds(pl.multiple_of(i * step, step), step)
            c = pl.ds(k * SLAB, SLAB)
            hg = (hg_own[r, c] + hgr[r, c].astype(F32)) * live
            dg_v[k, r, :] = (hg * fg[k, r, :]).astype(BF)
            du_v[k, r, :] = (hg * fu[k, r, :]).astype(BF)

    out_d = [local(11, dg_v, dg_out), local(12, du_v, du_out)]
    for c in out_d:
        c.start()

    rs_tick(7)

    for j, x_ in enumerate((x, x3, x1, x2)):
        for i in range(2):
            ref = mb.at[x_ * 2 + 1 - core, i]
            arrived(("mc", j, i), ref, cn)

    for k in range(2):
        total = gb[rows_of(z), sub(k)].astype(F32)
        for d in range(2):
            last = hops(d, k) - 1
            ref = rsb.at[d, last, :, sub(k)]
            arrived(("rs", d, last, k), ref, zn[d])
            total += ref[...].astype(F32)
        grad[:, sub(k)] = total * (TOK * 32) ** (-0.5)

    for k in range(CAP):
        q, j, n = slots[k]
        live = n.astype(F32)
        g = grad[:, pl.ds(k * SLAB, SLAB)]
        m = (LR1 * mb[q, 0, j].astype(F32) + 0.1 * g) * live
        s = (LR2 * mb[q, 1, j].astype(F32) + 0.05 * g * g) * live
        nf_v[k] = m
        ns_v[k] = s
        sd_v[k] = m / (1.0 - LR1**20) / (jnp.sqrt(s / (1.0 - LR2**20)) + 1e-08)

    out_m = [local(13, nf_v, nf_out), local(14, ns_v, ns_out), local(15, sd_v, sd_out)]
    for c in out_m:
        c.start()

    @pl.when(lo == 0)
    def _():
        for i in range(2):
            to_y(i).wait_send()

    for c in started:
        c.wait_send()
    for c in (*out_d, *out_m):
        c.wait()


def per_device(gate, up, og, w, m1, m2, old_map, new_map):
    hbm = pl.BlockSpec(memory_space=pl.ANY)
    vmem = pl.BlockSpec(memory_space=pltpu.VMEM)
    act = (CAP, TOK, SLAB)
    state = (CAP, ROWS, SLAB)
    old = (CAP_OLD, ROWS, SLAB)
    V = pltpu.VMEM
    outs = pl.pallas_call(
        body,
        out_shape=[jax.ShapeDtypeStruct(act, BF)] * 2 + [jax.ShapeDtypeStruct(state, F32)] * 3,
        in_specs=[hbm] * 6 + [vmem] * 2,
        out_specs=[hbm] * 5,
        scratch_shapes=[
            V(act, BF), V(act, BF), V(act, F32), V(act, F32), V(old, F32), V(old, F32),
            V((2 * TOK, HALF), BF), V((2 * TOK, COLS), BF),
            V((TOK, COLS), BF), V((TOK, COLS), BF), V((TOK, COLS), F32),
            V((HALF, COLS), BF), V((HALF, COLS), BF), V((2, HOPS, ROWS, COLS), BF),
            V((8, 2, *old), BF), V((ROWS, COLS), F32),
            V(act, BF), V(act, BF), V(state, F32), V(state, F32), V(state, F32),
            pltpu.SemaphoreType.DMA((len(SEM),)), pltpu.SemaphoreType.DMA((len(SEM),)),
            pltpu.SemaphoreType.DMA((16,)),
        ],
        compiler_params=pltpu.CompilerParams(
            collective_id=0, has_side_effects=True, vmem_limit_bytes=56 << 20
        ),
        cost_estimate=pl.CostEstimate(flops=6 * 10**9, bytes_accessed=12 * 10**6, transcendentals=0),
        name="step",
    )(
        gate[:, 0].transpose(1, 0, 2),
        up[:, 0].transpose(1, 0, 2),
        og,
        w[0].transpose(1, 0, 2),
        m1[0].transpose(1, 0, 2),
        m2[0].transpose(1, 0, 2),
        old_map[None],
        new_map[None],
    )
    dg, du, nf, ns, sd = outs
    return (
        dg.transpose(1, 0, 2)[:, None],
        du.transpose(1, 0, 2)[:, None],
        nf.transpose(1, 0, 2)[None],
        ns.transpose(1, 0, 2)[None],
        sd.transpose(1, 0, 2)[None],
    )


def solution(mesh):
    act, state = P("dp", "owner", None, None), P("owner", "dp", None, None)
    return jax.shard_map(
        per_device,
        mesh=mesh,
        in_specs=(act, act, P("dp", None), state, state, state, P(), P()),
        out_specs=(act, act, state, state, state),
        check_vma=False,
    )
```

time: 965 us -> 95.1 us (0.10)
  the two profiles are of different devices: /device:TPU:24 before, /device:TPU:32 now
where the time goes in v1:
time: 95.1 us; the launch traced here: 94.9 us
  Pallas kernels  88.2 us (93%)
  local copies, waits for them, and re-layouts  5.99 us (6%)
    pallas_call x1, Pallas kernels, per_device(): pl.pallas_call(body, out_shape=[jax.ShapeDtypeStruct(act, BF)] * 2 + [jax...  88.2 us
    unnamed x11, local copies, waits for them, and re-layouts  5.99 us

profile of v1, /device:TPU:32, one launch (start us, length us, event | category | flops | bytes accessed | tf_op | source)
XLA Modules:
  0.0 94.9 jit_solution(14441792200998832325)
XLA Ops:
  0.6 88.2 %step.1 = (bf16[6,384,128]{2,1,0:T(8,128)(2,1)}, bf16[6,384,128]{2,1,0:T(8,128)(2,1)}, f32[6,80,128]{2,1,0:T(8,128)}, f32[6,80,128]{2,1,0:T(8,128)}, f32[6,80,128]{2,1,0:T(8,128)}) custom-call(bf16[6,384,128]{2,1,0:T(8,128)(2,1)} %bitcast.37, bf16[6,384,128]{2,1,0:T(8,128)(2,1)} %bitcast.38, bf16[384,2560]{1,0:T(8,128)(2,1)} %og.1, ...), custom_call_target="tpu_custom_call" | custom-call | flops 6000000000 | bytes 12000000 | tf_op jit(solution)/shard_map/step/pallas_call | solution.py:385
  88.8 0.0 copy-start.2
  88.9 0.0 copy-start.1
  88.9 0.0 copy-start
  88.9 2.0 %copy.18 = bf16[384,1,6,128]{3,0,2,1:T(8,128)(2,1)} copy(bf16[384,1,6,128]{3,0,2,1:T(8,128)(2,1)} %bitcast.33) | data formatting | bytes 1179648
  90.9 1.9 %copy.19 = bf16[384,1,6,128]{3,0,2,1:T(8,128)(2,1)} copy(bf16[384,1,6,128]{3,0,2,1:T(8,128)(2,1)} %bitcast.32) | data formatting | bytes 1179648
  92.8 0.0 copy-done.2
  92.8 0.7 copy.20
  93.5 0.0 copy-done.1
  93.5 0.7 copy.21
  94.2 0.0 copy-done
  94.2 0.7 copy.22
Async XLA Ops:
  88.8 3.9 %copy-start.2 = (f32[6,80,128]{2,1,0:T(8,128)S(1)}, f32[6,80,128]{2,1,0:T(8,128)}, u32[]{:S(2)}) copy-start(f32[6,80,128]{2,1,0:T(8,128)} %get-tuple-element.12) | copy-start | bytes 737284
  88.9 4.6 %copy-start.1 = (f32[6,80,128]{2,1,0:T(8,128)S(1)}, f32[6,80,128]{2,1,0:T(8,128)}, u32[]{:S(2)}) copy-start(f32[6,80,128]{2,1,0:T(8,128)} %get-tuple-element.13) | copy-start | bytes 737284
  88.9 5.3 %copy-start = (f32[6,80,128]{2,1,0:T(8,128)S(1)}, f32[6,80,128]{2,1,0:T(8,128)}, u32[]{:S(2)}) copy-start(f32[6,80,128]{2,1,0:T(8,128)} %get-tuple-element.14) | copy-start | bytes 737284

commit v2 on v1

--- a/solution.py
+++ b/solution.py
@@ -16,37 +16,37 @@
 HALF = WIDTH // 2
 ROWS = WIDTH // 32
 COLS = CAP * SLAB
-SUB = COLS // 2
+SUBS = 3
+SUB = COLS // SUBS
 UNIT = TOK // 8
 GB = 256
 N_SLAB = 54
 LR1, LR2 = 0.9, 0.95
 
-SEM = {}
+RECV, SEND = {}, {}
 
 
 def _number(*names):
     for n in names:
-        SEM[n] = len(SEM)
+        RECV[n], SEND[n] = len(set(RECV.values())), len(set(SEND.values()))
 
 
 for _s in range(HOPS):
     for _d in range(2):
-        for _k in range(2):
-            _number(("ag", _d, _s, _k), ("rs", _d, _s, _k))
+        for _k in range(SUBS):
+            RECV["ag", _d, _s, _k] = RECV["rs", _d, _s, _k] = (_s * 2 + _d) * SUBS + _k
+            SEND["ag", _d, _s, _k] = (_s % 2 * 2 + _d) * SUBS + _k
+            SEND["rs", _d, _s, _k] = 4 * SUBS + (_s % 2 * 2 + _d) * SUBS + _k
 _number(("og",), ("ogx", 0), ("ogx", 1), ("ogx", 2), *[("ogc", i) for i in range(4)])
-for _r in range(2):
-    for _d in range(2):
-        _number(("hid", _d, _r), ("hg", _d, _r))
+_number(*[(n, r) for n in ("hid", "hg") for r in range(2)])
 for _i in range(2):
-    _number(("my", _i), ("mx", 0, _i), ("mx", 1, _i), ("mf", _i))
-    _number(*[("mc", j, _i) for j in range(4)])
+    _number(("my", _i), *[("mx", j, _i) for j in range(3)], *[("mc", j, _i) for j in range(4)])
 
 
 def body(
     gate, up, og, w, m1, m2, old_map, new_map,
     dg_out, du_out, nf_out, ns_out, sd_out,
-    gate_v, up_v, fg, fu, m1_v, m2_v, og_v, hid, hgs, hgr, hg_own,
+    gate_v, up_v, fg, fu, m1_v, m2_v, old_v, new_v, og_s, og_v, hid, hgs, hgr, hg_own,
     wb, gb, rsb, mb, grad, dg_v, du_v, nf_v, ns_v, sd_v,
     ssem, rsem, lsem,
 ):
@@ -62,22 +62,24 @@
     far = dev((y + 2) % NY, x, z, core)
     lows = dev((y // 2) * 2 + 1 - lo, x, z, core)
     xn = (dev(y, (x + 1) % NX, z, core), dev(y, (x + NX - 1) % NX, z, core))
+    across = dev(y, (x + 2) % NX, z, core)
     cn = dev(y, x, z, 1 - core)
     other = dev((y + NY - 1 + 2 * lo) % NY, x, z, core)
 
-    started = []
+    started = {}
 
     def copy(name, src, dst, device):
-        i = SEM[name]
         return pltpu.make_async_remote_copy(
-            src_ref=src, dst_ref=dst, send_sem=ssem.at[i], recv_sem=rsem.at[i],
+            src_ref=src, dst_ref=dst, send_sem=ssem.at[SEND[name]], recv_sem=rsem.at[RECV[name]],
             device_id=device, device_id_type=MESH,
         )
 
     def send(name, src, dst, device):
-        c = copy(name, src, dst, device)
-        c.start()
-        started.append(c)
+        i = SEND[name]
+        if i in started:
+            started[i].wait_send()
+        started[i] = copy(name, src, dst, device)
+        started[i].start()
 
     def arrived(name, dst, device):
         copy(name, dst, dst, device).wait_recv()
@@ -93,35 +95,39 @@
 
     mine_d = pl.ds(pl.multiple_of(hi * HALF, 128), HALF)
     other_d = pl.ds(pl.multiple_of((1 - hi) * HALF, 128), HALF)
+
+    def unit(x_, c_):
+        return pl.ds(pl.multiple_of((x_ * 2 + c_) * UNIT, 16), UNIT)
+
+    barrier = pltpu.get_barrier_semaphore()
+    for n in (*zn, *xn, cn, far, other, lows, across):
+        pl.semaphore_signal(barrier, inc=1, device_id=n, device_id_type=MESH)
 
     loads_w = [local(i, w.at[i], wb.at[rows_of(z), pl.ds(i * SLAB, SLAB)]) for i in range(CAP)]
     load_gate, load_up = local(6, gate, gate_v), local(7, up, up_v)
     load_og = local(8, og.at[:, mine_d], og_v.at[pl.ds(0, TOK)])
     load_m = [local(9, m1, m1_v), local(10, m2, m2_v)]
-    for c in [*loads_w, load_gate, load_up, load_og, *load_m]:
+    load_map = [local(16, old_map, old_v), local(17, new_map, new_v)]
+    load_unit = local(18, og.at[unit(x, core), other_d], og_s)
+    for c in [load_unit, *loads_w, load_gate, load_up, load_og, *load_m, *load_map]:
         c.start()
 
-    barrier = pltpu.get_barrier_semaphore()
-    for n in (*zn, *xn, cn, far, other, lows):
-        pl.semaphore_signal(barrier, inc=1, device_id=n, device_id_type=MESH)
-    pl.semaphore_wait(barrier, 8)
-
-    def unit(x_, c_):
-        return pl.ds(pl.multiple_of((x_ * 2 + c_) * UNIT, 16), UNIT)
+    pl.semaphore_wait(barrier, 9)
 
     def og_part(x_, c_):
         return og_v.at[pl.ds(pl.multiple_of(TOK + (x_ * 2 + c_) * UNIT, 16), UNIT)]
 
-    send(("og",), og.at[unit(x, core), other_d], og_part(x, core), other)
+    load_unit.wait()
+    send(("og",), og_s, og_part(x, core), other)
 
     def hops(d, k):
-        return HOPS if d == k else HOPS - 1
+        return HOPS if d == k % 2 else HOPS - 1
 
     def ag_slot(d, s):
         return (z + NZ - s) % NZ if d == 0 else (z + s) % NZ
 
     def ag_tick(s):
-        for k in range(2):
+        for k in range(SUBS):
             for d in range(2):
                 if 0 < s <= hops(d, k):
                     dst = wb.at[rows_of(ag_slot(d, s)), sub(k)]
@@ -135,7 +141,7 @@
         return (z + n - s) % NZ if d == 0 else (z + NZ - n + s) % NZ
 
     def rs_tick(s):
-        for k in range(2):
+        for k in range(SUBS):
             for d in range(2):
                 if s >= hops(d, k):
                     continue
@@ -178,17 +184,37 @@
 
     for r in range(2):
         hidden_rows(r * (TOK // 2))
-        for d in range(2):
-            send(("hid", d, r), hid.at[half(r), sub(d)], hid.at[partner(r), sub(d)], far)
-
+
+    def og_to(name, x_, device):
+        send(name, og_part(x_, core), og_part(x_, core), device)
+
+    arrived(("og",), og_part(x, core), other)
+    for j, device in enumerate((*xn, across)):
+        og_to(("ogx", j), x, device)
+    og_to(("ogc", 0), x, cn)
+    for r in range(2):
+        send(("hid", r), hid.at[half(r)], hid.at[partner(r)], far)
+
+    ag_tick(1)
+    ag_tick(2)
+    ag_tick(3)
+
+    x1, x2, x3 = (x + 1) % NX, (x + 2) % NX, (x + 3) % NX
     me = x * 2 + core
 
-    for c in load_m:
+    def mom(x_, i):
+        return mb.at[x_ * 2 + core, i]
+
+    def mom_copies():
+        copies = []
+        for j, device in enumerate((*xn, across)):
+            copies += [copy(("mx", j, i), mom(x, i), mom(x, i), device) for i in range(2)]
+        return copies + [copy(("mc", 0, i), mom(x, i), mom(x, i), cn) for i in range(2)]
+
+    mom_y = [copy(("my", i), mom(x, i), mom(x, i), lows) for i in range(2)]
+
+    for c in (*load_m, *load_map):
         c.wait()
-
-    def to_y(i):
-        ref = mb.at[me, i]
-        return copy(("my", i), ref, ref, lows)
 
     @pl.when(lo == 0)
     def _():
@@ -197,56 +223,25 @@
             mb[me, 0, j] = m1_v[j].astype(BF)
             mb[me, 1, j] = m2_v[j].astype(BF)
 
-        for i in range(2):
-            to_y(i).start()
-
-    ag_tick(1)
-
-    def og_to(name, x_, device):
-        send(name, og_part(x_, core), og_part(x_, core), device)
-
-    x1, x2, x3 = (x + 1) % NX, (x + 2) % NX, (x + 3) % NX
-    arrived(("og",), og_part(x, core), other)
-    og_to(("ogx", 0), x, xn[0])
-    og_to(("ogx", 1), x, xn[1])
-    og_to(("ogc", 0), x, cn)
-
-    ag_tick(2)
-
-    arrived(("ogx", 0), og_part(x3, core), xn[0])
-    og_to(("ogx", 2), x3, xn[0])
-    og_to(("ogc", 1), x3, cn)
-    arrived(("ogx", 1), og_part(x1, core), xn[1])
-    og_to(("ogc", 2), x1, cn)
-
-    ag_tick(3)
-
-    @pl.when(lo == 1)
+        for c in mom_copies():
+            c.start()
+
+    for j, x_ in enumerate((x3, x1, x2)):
+        arrived(("ogx", j), og_part(x_, core), xn[0])
+        og_to(("ogc", j + 1), x_, cn)
+    ag_tick(4)
+    ag_tick(5)
+    for r in range(2):
+        arrived(("hid", r), hid.at[partner(r)], far)
+
+    @pl.when(lo == 0)
     def _():
-        for i in range(2):
-            to_y(i).wait_recv()
-
-    def mom(x_, i):
-        return mb.at[x_ * 2 + core, i]
-
-    def mom_to(name, x_, i, device):
-        send(name, mom(x_, i), mom(x_, i), device)
-
-    for i in range(2):
-        for d in range(2):
-            mom_to(("mx", d, i), x, i, xn[d])
-        mom_to(("mc", 0, i), x, i, cn)
-
-    ag_tick(4)
-    arrived(("ogx", 2), og_part(x2, core), xn[0])
-    og_to(("ogc", 3), x2, cn)
-    ag_tick(5)
-    for i, x_ in enumerate((x, x3, x1, x2)):
-        arrived(("ogc", i), og_part(x_, 1 - core), cn)
+        for c in mom_y:
+            c.start()
+
+    for j, x_ in enumerate((x, x3, x1, x2)):
+        arrived(("ogc", j), og_part(x_, 1 - core), cn)
     load_og.wait()
-    for r in range(2):
-        for d in range(2):
-            arrived(("hid", d, r), hid.at[partner(r), sub(d)], far)
 
     def grad_block(i):
         part = lax.dot_general(
@@ -256,21 +251,15 @@
         gb[pl.ds(i * GB, GB), :] = part.astype(BF)
 
     grad_block(0)
+    grad_block(1)
     ag_tick(6)
-    grad_block(1)
     grad_block(2)
-    ag_tick(7)
     grad_block(3)
     grad_block(4)
     rs_tick(0)
+    ag_tick(7)
+    rs_tick(1)
     ag_tick(8)
-
-    for d, x_ in enumerate((x3, x1)):
-        for i in range(2):
-            arrived(("mx", d, i), mom(x_, i), xn[d])
-        mom_to(("mf", d), x_, d, xn[d])
-        for i in range(2):
-            mom_to(("mc", 1 + d, i), x_, i, cn)
 
     def hidden_grad(first, out):
         @pl.loop(0, 3)
@@ -282,10 +271,18 @@
 
     hidden_grad(TOK, hgs)
     for r in range(2):
-        for d in range(2):
-            send(("hg", d, r), hgs.at[half(r), sub(d)], hgr.at[half(r), sub(d)], far)
-    rs_tick(1)
+        send(("hg", r), hgs.at[half(r)], hgr.at[half(r)], far)
+    rs_tick(2)
     hidden_grad(0, hg_own)
+
+    @pl.when(lo == 1)
+    def _():
+        for c in mom_y:
+            c.wait_recv()
+        for c in mom_copies():
+            c.start()
+
+    rs_tick(3)
 
     same = (N_SLAB, N_SLAB)
     lane, row = lax.broadcasted_iota(jnp.int32, same, 1), lax.broadcasted_iota(jnp.int32, same, 0)
@@ -297,8 +294,8 @@
         rank = jnp.sum(jnp.where((across == down) & earlier, 1, 0), axis=0, keepdims=True)
         return ref[...], rank
 
-    old_own, old_rank = owners_ranks(old_map)
-    new_own, new_rank = owners_ranks(new_map)
+    old_own, old_rank = owners_ranks(old_v)
+    new_own, new_rank = owners_ranks(new_v)
     slots = []
     for k in range(CAP):
         here = (new_own == ow) & (new_rank == k)
@@ -306,19 +303,17 @@
             tuple(jnp.sum(jnp.where(here, v, 0)) for v in (old_own, old_rank, jnp.ones_like(old_own)))
         )
 
-    rs_tick(2)
-
-    rs_tick(3)
-    for d in range(2):
-        arrived(("mf", d), mom(x2, d), xn[d])
-        mom_to(("mc", 3, d), x2, d, cn)
     rs_tick(4)
     rs_tick(5)
-    rs_tick(6)
+    for j, x_ in enumerate((x3, x1, x2)):
+        if j == 2:
+            rs_tick(6)
+        for i in range(2):
+            arrived(("mx", j, i), mom(x_, i), xn[0])
+            send(("mc", j + 1, i), mom(x_, i), mom(x_, i), cn)
 
     for r in range(2):
-        for d in range(2):
-            arrived(("hg", d, r), hgr.at[half(r), sub(d)], far)
+        arrived(("hg", r), hgr.at[half(r)], far)
     for k in range(CAP):
         live = slots[k][2].astype(F32)
 
@@ -341,7 +336,7 @@
             ref = mb.at[x_ * 2 + 1 - core, i]
             arrived(("mc", j, i), ref, cn)
 
-    for k in range(2):
+    for k in range(SUBS):
         total = gb[rows_of(z), sub(k)].astype(F32)
         for d in range(2):
             last = hops(d, k) - 1
@@ -366,18 +361,30 @@
 
     @pl.when(lo == 0)
     def _():
-        for i in range(2):
-            to_y(i).wait_send()
-
-    for c in started:
+        for c in mom_y:
+            c.wait_send()
+
+    for c in (*started.values(), *mom_copies()):
         c.wait_send()
     for c in (*out_d, *out_m):
         c.wait()
 
 
+def write_out(*refs):
+    src, dst, held, sem = refs[:5], refs[5:10], refs[10:15], refs[15]
+    first = [pltpu.make_async_copy(src[i], held[i], sem.at[i]) for i in range(5)]
+    second = [pltpu.make_async_copy(held[i], dst[i], sem.at[5 + i]) for i in range(5)]
+    for c in first:
+        c.start()
+    for a, b in zip(first, second):
+        a.wait()
+        b.start()
+    for c in second:
+        c.wait()
+
+
 def per_device(gate, up, og, w, m1, m2, old_map, new_map):
     hbm = pl.BlockSpec(memory_space=pl.ANY)
-    vmem = pl.BlockSpec(memory_space=pltpu.VMEM)
     act = (CAP, TOK, SLAB)
     state = (CAP, ROWS, SLAB)
     old = (CAP_OLD, ROWS, SLAB)
@@ -385,17 +392,18 @@
     outs = pl.pallas_call(
         body,
         out_shape=[jax.ShapeDtypeStruct(act, BF)] * 2 + [jax.ShapeDtypeStruct(state, F32)] * 3,
-        in_specs=[hbm] * 6 + [vmem] * 2,
+        in_specs=[hbm] * 8,
         out_specs=[hbm] * 5,
         scratch_shapes=[
-            V(act, BF), V(act, BF), V(act, F32), V(act, F32), V(old, F32), V(old, F32),
-            V((2 * TOK, HALF), BF), V((2 * TOK, COLS), BF),
+            V(act, BF), V(act, BF), V(act, F32), V(act, F32), V(old, F32), V(old, F32), V((1, N_SLAB), jnp.int32), V((1, N_SLAB), jnp.int32),
+            V((UNIT, HALF), BF), V((2 * TOK, HALF), BF), V((2 * TOK, COLS), BF),
             V((TOK, COLS), BF), V((TOK, COLS), BF), V((TOK, COLS), F32),
             V((HALF, COLS), BF), V((HALF, COLS), BF), V((2, HOPS, ROWS, COLS), BF),
             V((8, 2, *old), BF), V((ROWS, COLS), F32),
             V(act, BF), V(act, BF), V(state, F32), V(state, F32), V(state, F32),
-            pltpu.SemaphoreType.DMA((len(SEM),)), pltpu.SemaphoreType.DMA((len(SEM),)),
-            pltpu.SemaphoreType.DMA((16,)),
+            pltpu.SemaphoreType.DMA((len(set(SEND.values())),)),
+            pltpu.SemaphoreType.DMA((len(set(RECV.values())),)),
+            pltpu.SemaphoreType.DMA((19,)),
         ],
         compiler_params=pltpu.CompilerParams(
             collective_id=0, has_side_effects=True, vmem_limit_bytes=56 << 20
@@ -412,7 +420,14 @@
         old_map[None],
         new_map[None],
     )
-    dg, du, nf, ns, sd = outs
+    dg, du, nf, ns, sd = pl.pallas_call(
+        write_out,
+        out_shape=[jax.ShapeDtypeStruct(o.shape, o.dtype) for o in outs],
+        in_specs=[hbm] * 5,
+        out_specs=[hbm] * 5,
+        scratch_shapes=[*[V(o.shape, o.dtype) for o in outs], pltpu.SemaphoreType.DMA((10,))],
+        name="write_out",
+    )(*outs)
     return (
         dg.transpose(1, 0, 2)[:, None],
         du.transpose(1, 0, 2)[:, None],

time: 95.1 us -> 72.8 us (0.77)
  the two profiles are of different devices: /device:TPU:32 before, /device:TPU:8 now
where the time goes in v2:
time: 72.8 us; the launch traced here: 72.7 us
  Pallas kernels  72 us (99%)
    pallas_call x1, Pallas kernels, per_device(): pl.pallas_call(body, out_shape=[jax.ShapeDtypeStruct(act, BF)] * 2 + [jax...  69.6 us
    pallas_call x1, Pallas kernels, per_device(): pl.pallas_call(write_out, out_shape=[jax.ShapeDtypeStruct(o.shape, o.dtyp...  2.4 us

profile of v2, /device:TPU:8, one launch (start us, length us, event | category | flops | bytes accessed | tf_op | source)
XLA Modules:
  0.0 72.7 jit_solution(6939005683183538636)
XLA Ops:
  0.6 69.6 %step.1 = (bf16[6,384,128]{2,1,0:T(8,128)(2,1)}, bf16[6,384,128]{2,1,0:T(8,128)(2,1)}, f32[6,80,128]{2,1,0:T(8,128)}, f32[6,80,128]{2,1,0:T(8,128)}, f32[6,80,128]{2,1,0:T(8,128)}) custom-call(bf16[6,384,128]{2,1,0:T(8,128)(2,1)} %bitcast.32, bf16[6,384,128]{2,1,0:T(8,128)(2,1)} %bitcast.33, bf16[384,2560]{1,0:T(8,128)(2,1)} %og.1, ...), custom_call_target="tpu_custom_call" | custom-call | flops 6000000000 | bytes 12000000 | tf_op jit(solution)/shard_map/step/pallas_call | solution.py:392
  70.3 2.4 %write_out.1 = (bf16[6,384,128]{2,1,0:T(8,128)(2,1)}, bf16[6,384,128]{2,1,0:T(8,128)(2,1)}, f32[6,80,128]{2,1,0:T(8,128)}, f32[6,80,128]{2,1,0:T(8,128)}, f32[6,80,128]{2,1,0:T(8,128)}) custom-call(bf16[6,384,128]{2,1,0:T(8,128)(2,1)} %get-tuple-element.15.refs_0_, bf16[6,384,128]{2,1,0:T(8,128)(2,1)} %get-tuple-element.16.refs_1_, ...), custom_call_target="tpu_custom_call" | custom-call | tf_op jit(solution)/shard_map/write_out/pallas_call | solution.py:423

commit v3 on v2

v3 whole, which is shorter than its diff:
```python
import functools

import jax
import jax.numpy as jnp
from jax import lax
from jax.experimental import pallas as pl
from jax.experimental.pallas import tpu as pltpu
from jax.sharding import PartitionSpec as P

MESH = pl.DeviceIdType.MESH
BF, F32 = jnp.bfloat16, jnp.float32
NZ, NY, NX = 16, 4, 4
HOPS = 8
CAP, CAP_OLD, SLAB = 6, 9, 128
TOK, WIDTH = 384, 2560
HALF = WIDTH // 2
ROWS = WIDTH // 32
COLS = CAP * SLAB
SUBS = 3
SUB = COLS // SUBS
UNIT = TOK // 8
GB = 256
N_SLAB = 54
LR1, LR2 = 0.9, 0.95

RECV, SEND = {}, {}


def _number(*names):
    for n in names:
        RECV[n], SEND[n] = len(set(RECV.values())), len(set(SEND.values()))


for _s in range(HOPS):
    for _d in range(2):
        for _k in range(SUBS):
            RECV["ag", _d, _s, _k] = RECV["rs", _d, _s, _k] = (_s * 2 + _d) * SUBS + _k
            SEND["ag", _d, _s, _k] = (_s % 2 * 2 + _d) * SUBS + _k
            SEND["rs", _d, _s, _k] = 4 * SUBS + (_s % 2 * 2 + _d) * SUBS + _k
_number(("og",), ("ogx", 0), ("ogx", 1), ("ogx", 2), *[("ogc", i) for i in range(4)])
_number(*[(n, k) for n in ("hid", "hg") for k in range(SUBS)])
for _i in range(2):
    _number(("my", _i), *[("mx", j, _i) for j in range(3)], *[("mc", j, _i) for j in range(4)])


def body(
    gate, up, og, w, m1, m2, old_map, new_map,
    dg_v, du_v, nf_v, ns_v, sd_v,
    gate_v, up_v, fg, fu, m1_v, m2_v, old_v, new_v, og_s, og_v, ogt, hid, hgs, hgr, hg_own,
    wb, gb, rsb, mb, grad,
    ssem, rsem, lsem,
):
    dp, ow = lax.axis_index("dp"), lax.axis_index("owner")
    hi, z = dp // NZ, dp % NZ
    lo, x, core = ow // 8, (ow // 2) % NX, ow % 2
    y = hi * 2 + lo

    def dev(y_, x_, z_, c_):
        return ((y_ // 2) * NZ + z_, (y_ % 2) * 8 + x_ * 2 + c_)

    zn = (dev(y, x, (z + 1) % NZ, core), dev(y, x, (z + NZ - 1) % NZ, core))
    far = dev((y + 2) % NY, x, z, core)
    lows = dev((y // 2) * 2 + 1 - lo, x, z, core)
    xn = (dev(y, (x + 1) % NX, z, core), dev(y, (x + NX - 1) % NX, z, core))
    across = dev(y, (x + 2) % NX, z, core)
    cn = dev(y, x, z, 1 - core)
    other = dev((y + NY - 1 + 2 * lo) % NY, x, z, core)

    started = {}

    def copy(name, src, dst, device):
        return pltpu.make_async_remote_copy(
            src_ref=src, dst_ref=dst, send_sem=ssem.at[SEND[name]], recv_sem=rsem.at[RECV[name]],
            device_id=device, device_id_type=MESH,
        )

    def send(name, src, dst, device):
        i = SEND[name]
        if i in started:
            started[i].wait_send()
        started[i] = copy(name, src, dst, device)
        started[i].start()

    def arrived(name, dst, device):
        copy(name, dst, dst, device).wait_recv()

    def local(i, src, dst):
        return pltpu.make_async_copy(src, dst, lsem.at[i])

    def rows_of(t):
        return pl.ds(pl.multiple_of(t * ROWS, 16), ROWS)

    def sub(k):
        return pl.ds(k * SUB, SUB)

    mine_d = pl.ds(pl.multiple_of(hi * HALF, 128), HALF)
    other_d = pl.ds(pl.multiple_of((1 - hi) * HALF, 128), HALF)

    def unit(x_, c_):
        return pl.ds(pl.multiple_of((x_ * 2 + c_) * UNIT, 16), UNIT)

    barrier = pltpu.get_barrier_semaphore()
    for n in (*zn, *xn, cn, far, other, lows, across):
        pl.semaphore_signal(barrier, inc=1, device_id=n, device_id_type=MESH)

    loads_w = [local(i, w.at[i], wb.at[rows_of(z), pl.ds(i * SLAB, SLAB)]) for i in range(CAP)]
    load_gate, load_up = local(6, gate, gate_v), local(7, up, up_v)
    load_og = local(8, og.at[:, mine_d], og_v.at[pl.ds(0, TOK)])
    load_m = [local(9, m1, m1_v), local(10, m2, m2_v)]
    load_map = [local(16, old_map, old_v), local(17, new_map, new_v)]
    load_unit = local(18, og.at[unit(x, core), other_d], og_s)
    for c in [load_unit, *loads_w, load_gate, load_up, load_og, *load_m, *load_map]:
        c.start()

    pl.semaphore_wait(barrier, 9)

    def og_part(x_, c_):
        return og_v.at[pl.ds(pl.multiple_of(TOK + (x_ * 2 + c_) * UNIT, 16), UNIT)]

    load_unit.wait()
    send(("og",), og_s, og_part(x, core), other)

    def hops(d, k):
        return HOPS if d == k % 2 else HOPS - 1

    def ag_slot(d, s):
        return (z + NZ - s) % NZ if d == 0 else (z + s) % NZ

    def ag(s, *parts):
        for k in parts or range(SUBS):
            for d in range(2):
                if s > hops(d, k):
                    continue
                ref = wb.at[rows_of(ag_slot(d, s)), sub(k)]
                if s > 0:
                    arrived(("ag", d, s - 1, k), ref, zn[d])
                if s < hops(d, k):
                    send(("ag", d, s, k), ref, ref, zn[d])

    def rs_dest(d, s, k):
        n = hops(d, k)
        return (z + n - s) % NZ if d == 0 else (z + NZ - n + s) % NZ

    def rs(s, k):
        for d in range(2):
            n = hops(d, k)
            if s > n:
                continue
            if s == 0:
                src = gb.at[rows_of(rs_dest(d, s, k)), sub(k)]
            else:
                src = rsb.at[d, s - 1, :, sub(k)]
                arrived(("rs", d, s - 1, k), src, zn[d])
                if s == n:
                    continue
                mine = gb[rows_of(rs_dest(d, s, k)), sub(k)]
                src[...] = (src[...].astype(F32) + mine.astype(F32)).astype(BF)
            send(("rs", d, s, k), src, rsb.at[d, s, :, sub(k)], zn[d])

    def rs_sum(k):
        total = gb[rows_of(z), sub(k)].astype(F32)
        for d in range(2):
            total += rsb[d, hops(d, k) - 1, :, sub(k)].astype(F32)
        grad[:, sub(k)] = total * (TOK * 32) ** (-0.5)

    for c in loads_w:
        c.wait()
    ag(0, 0)

    load_gate.wait()
    load_up.wait()
    step = 64

    for slot in range(CAP):

        @pl.loop(0, TOK // step)
        def _(i):
            r = pl.ds(pl.multiple_of(i * step, step), step)
            g = gate_v[slot, r, :].astype(F32)
            u = up_v[slot, r, :].astype(F32)
            sig = jax.nn.sigmoid(g)
            gs = g * sig
            hid[r, pl.ds(slot * SLAB, SLAB)] = (gs * u).astype(BF)
            fu[slot, r, :] = gs
            fg[slot, r, :] = u * sig * (1.0 + g * (1.0 - sig))

    own, theirs = pl.ds(0, TOK), pl.ds(TOK, TOK)

    def hid_to(k):
        send(("hid", k), hid.at[own, sub(k)], hid.at[theirs, sub(k)], far)

    def turn(tokens):
        for i in range(HALF // GB):
            ogt[pl.ds(i * GB, GB), tokens] = og_v[tokens, pl.ds(i * GB, GB)].T

    ag(0, 1)
    load_og.wait()
    turn(own)

    x1, x2, x3 = (x + 1) % NX, (x + 2) % NX, (x + 3) % NX
    me = x * 2 + core

    def mom(x_, i):
        return mb.at[x_ * 2 + core, i]

    def mom_copies():
        copies = []
        for j, device in enumerate((*xn, across)):
            copies += [copy(("mx", j, i), mom(x, i), mom(x, i), device) for i in range(2)]
        return copies + [copy(("mc", 0, i), mom(x, i), mom(x, i), cn) for i in range(2)]

    mom_y = [copy(("my", i), mom(x, i), mom(x, i), lows) for i in range(2)]

    for c in (*load_m, *load_map):
        c.wait()

    @pl.when(lo == 0)
    def _():
        @pl.loop(0, CAP_OLD)
        def _(j):
            mb[me, 0, j] = m1_v[j].astype(BF)
            mb[me, 1, j] = m2_v[j].astype(BF)

    ag(0, 2)

    def og_to(name, x_, device):
        send(name, og_part(x_, core), og_part(x_, core), device)

    ag(1, 0)
    arrived(("og",), og_part(x, core), other)
    for j, device in enumerate((*xn, across)):
        og_to(("ogx", j), x, device)
    og_to(("ogc", 0), x, cn)
    hid_to(0)
    ag(1, 1, 2)
    ag(2)
    hid_to(1)
    ag(3, 0)
    for j, x_ in enumerate((x3, x1, x2)):
        arrived(("ogx", j), og_part(x_, core), xn[0])
        og_to(("ogc", j + 1), x_, cn)

    @pl.when(lo == 0)
    def _():
        for c in mom_copies():
            c.start()

    ag(3, 1, 2)
    hid_to(2)
    for j, x_ in enumerate((x, x3, x1, x2)):
        arrived(("ogc", j), og_part(x_, 1 - core), cn)
    turn(theirs)

    def gradient(k):
        arrived(("hid", k), hid.at[theirs, sub(k)], far)

        @pl.loop(0, 2)
        def _(i):
            r = pl.ds(pl.multiple_of(i * (HALF // 2), 128), HALF // 2)
            gb[r, sub(k)] = jnp.dot(
                ogt[r, :], hid[:, sub(k)], preferred_element_type=F32
            ).astype(BF)

    def mom_y_start(i):
        @pl.when(lo == 0)
        def _():
            mom_y[i].start()

    gradient(0)
    rs(0, 0)
    mom_y_start(0)
    ag(4)
    gradient(1)
    rs(1, 0)
    rs(0, 1)
    mom_y_start(1)
    ag(5)
    gradient(2)
    rs(2, 0)
    rs(1, 1)
    rs(0, 2)
    ag(6)
    rs(1, 2)
    rs(3, 0)
    ag(7)
    rs(2, 2)
    rs(2, 1)

    @pl.when(lo == 1)
    def _():
        for c in mom_y:
            c.wait_recv()
        for c in mom_copies():
            c.start()

    def hidden_grad(tokens, k, out):
        out[:, sub(k)] = jnp.dot(
            og_v[tokens, :], wb[:, sub(k)], preferred_element_type=F32
        ).astype(out.dtype)

    for k in range(SUBS):
        ag(8, k)
        hidden_grad(theirs, k, hgs)
        send(("hg", k), hgs.at[:, sub(k)], hgr.at[:, sub(k)], far)
    rs(3, 2)
    rs(3, 1)
    hidden_grad(own, 0, hg_own)

    same = (N_SLAB, N_SLAB)
    lane, row = lax.broadcasted_iota(jnp.int32, same, 1), lax.broadcasted_iota(jnp.int32, same, 0)
    diagonal, earlier = lane == row, row < lane

    def owners_ranks(ref):
        across = jnp.broadcast_to(ref[...], same)
        down = jnp.sum(jnp.where(diagonal, across, 0), axis=1, keepdims=True)
        rank = jnp.sum(jnp.where((across == down) & earlier, 1, 0), axis=0, keepdims=True)
        return ref[...], rank

    old_own, old_rank = owners_ranks(old_v)
    new_own, new_rank = owners_ranks(new_v)
    slots = []
    for k in range(CAP):
        here = (new_own == ow) & (new_rank == k)
        slots.append(
            tuple(jnp.sum(jnp.where(here, v, 0)) for v in (old_own, old_rank, jnp.ones_like(old_own)))
        )

    for k in range(SUBS):
        rs(4, k)
    hidden_grad(own, 1, hg_own)

    def mom_on(j, x_):
        for i in range(2):
            arrived(("mx", j, i), mom(x_, i), xn[0])
            send(("mc", j + 1, i), mom(x_, i), mom(x_, i), cn)

    for k in range(SUBS):
        rs(5, k)
    hidden_grad(own, 2, hg_own)
    mom_on(0, x3)
    mom_on(1, x1)

    def cotangents(part):
        arrived(("hg", part), hgr.at[:, sub(part)], far)
        for k in range(part * CAP // SUBS, (part + 1) * CAP // SUBS):
            live = slots[k][2].astype(F32)

            @pl.loop(0, TOK // step)
            def _(i):
                r = pl.ds(pl.multiple_of(i * step, step), step)
                c = pl.ds(k * SLAB, SLAB)
                hg = (hg_own[r, c] + hgr[r, c].astype(F32)) * live
                dg_v[k, r, :] = (hg * fg[k, r, :]).astype(BF)
                du_v[k, r, :] = (hg * fu[k, r, :]).astype(BF)

    for k in range(SUBS):
        rs(6, k)
    mom_on(2, x2)
    cotangents(0)
    for k in range(SUBS):
        rs(7, k)
    cotangents(1)
    cotangents(2)
    def adam(part):
        for k in range(part * CAP // SUBS, (part + 1) * CAP // SUBS):
            q, j, n = slots[k]
            live = n.astype(F32)
            g = grad[:, pl.ds(k * SLAB, SLAB)]
            m = (LR1 * mb[q, 0, j].astype(F32) + 0.1 * g) * live
            s = (LR2 * mb[q, 1, j].astype(F32) + 0.05 * g * g) * live
            nf_v[k] = m
            ns_v[k] = s
            sd_v[k] = m / (1.0 - LR1**20) / (jnp.sqrt(s / (1.0 - LR2**20)) + 1e-08)

    for j, x_ in enumerate((x, x3, x1, x2)):
        for i in range(2):
            ref = mb.at[x_ * 2 + 1 - core, i]
            arrived(("mc", j, i), ref, cn)
    for k in range(SUBS):
        rs(8, k)
        rs_sum(k)
        adam(k)

    @pl.when(lo == 0)
    def _():
        for c in mom_y:
            c.wait_send()

    for c in (*started.values(), *mom_copies()):
        c.wait_send()


def write_out(*refs):
    src, dst, sem = refs[:5], refs[5:10], refs[10]
    copies = [pltpu.make_async_copy(src[i], dst[i], sem.at[i]) for i in range(5)]
    for c in copies:
        c.start()
    for c in copies:
        c.wait()


def per_device(gate, up, og, w, m1, m2, old_map, new_map):
    hbm = pl.BlockSpec(memory_space=pl.ANY)
    act = (CAP, TOK, SLAB)
    state = (CAP, ROWS, SLAB)
    old = (CAP_OLD, ROWS, SLAB)
    V = pltpu.VMEM
    outs = pl.pallas_call(
        body,
        out_shape=[V(act, BF)] * 2 + [V(state, F32)] * 3,
        in_specs=[hbm] * 8,
        out_specs=[pl.BlockSpec(memory_space=V)] * 5,
        scratch_shapes=[
            V(act, BF), V(act, BF), V(act, F32), V(act, F32), V(old, F32), V(old, F32), V((1, N_SLAB), jnp.int32), V((1, N_SLAB), jnp.int32),
            V((UNIT, HALF), BF), V((2 * TOK, HALF), BF), V((HALF, 2 * TOK), BF), V((2 * TOK, COLS), BF),
            V((TOK, COLS), BF), V((TOK, COLS), BF), V((TOK, COLS), F32),
            V((HALF, COLS), BF), V((HALF, COLS), BF), V((2, HOPS, ROWS, COLS), BF),
            V((8, 2, *old), BF), V((ROWS, COLS), F32),
            pltpu.SemaphoreType.DMA((len(set(SEND.values())),)),
            pltpu.SemaphoreType.DMA((len(set(RECV.values())),)),
            pltpu.SemaphoreType.DMA((19,)),
        ],
        compiler_params=pltpu.CompilerParams(
            collective_id=0, has_side_effects=True, vmem_limit_bytes=40 << 20
        ),
        cost_estimate=pl.CostEstimate(flops=6 * 10**9, bytes_accessed=12 * 10**6, transcendentals=0),
        name="step",
    )(*[pltpu.with_memory_space_constraint(v, pltpu.HBM) for v in (
        gate[:, 0].transpose(1, 0, 2),
        up[:, 0].transpose(1, 0, 2),
        og,
        w[0].transpose(1, 0, 2),
        m1[0].transpose(1, 0, 2),
        m2[0].transpose(1, 0, 2),
        old_map[None],
        new_map[None],
    )])
    dg, du, nf, ns, sd = pl.pallas_call(
        write_out,
        out_shape=[jax.ShapeDtypeStruct(o.shape, o.dtype) for o in outs],
        in_specs=[pl.BlockSpec(memory_space=V)] * 5,
        out_specs=[hbm] * 5,
        scratch_shapes=[pltpu.SemaphoreType.DMA((5,))],
        name="write_out",
    )(*[pltpu.with_memory_space_constraint(o, V) for o in outs])
    return (
        dg.transpose(1, 0, 2)[:, None],
        du.transpose(1, 0, 2)[:, None],
        nf.transpose(1, 0, 2)[None],
        ns.transpose(1, 0, 2)[None],
        sd.transpose(1, 0, 2)[None],
    )


def solution(mesh):
    act, state = P("dp", "owner", None, None), P("owner", "dp", None, None)
    return jax.shard_map(
        per_device,
        mesh=mesh,
        in_specs=(act, act, P("dp", None), state, state, state, P(), P()),
        out_specs=(act, act, state, state, state),
        check_vma=False,
    )
```

time: 72.8 us -> 70.9 us (0.974)
  the two profiles are of different devices: /device:TPU:8 before, /device:TPU:24 now
where the time goes in v3:
time: 70.9 us; the launch traced here: 70.7 us
  Pallas kernels  70.1 us (99%)
    pallas_call x1, Pallas kernels, per_device(): pl.pallas_call(body, out_shape=[V(act, BF)] * 2 + [V(state, F32)] * 3, in...  68.8 us

profile of v3, /device:TPU:24, one launch (start us, length us, event | category | flops | bytes accessed | tf_op | source)
XLA Modules:
  0.0 70.7 jit_solution(2116409207198460156)
XLA Ops:
  0.6 68.8 %step.1 = (bf16[6,384,128]{2,1,0:T(8,128)(2,1)S(1)}, bf16[6,384,128]{2,1,0:T(8,128)(2,1)S(1)}, f32[6,80,128]{2,1,0:T(8,128)S(1)}, f32[6,80,128]{2,1,0:T(8,128)S(1)}, f32[6,80,128]{2,1,0:T(8,128)S(1)}) custom-call(bf16[6,384,128]{2,1,0:T(8,128)(2,1)} %bitcast.32, bf16[6,384,128]{2,1,0:T(8,128)(2,1)} %bitcast.33, bf16[384,2560]{1,0:T(8,128)(2,1)} %og.1, ...), custom_call_target="tpu_custom_call" | custom-call | flops 6000000000 | bytes 12000000 | tf_op jit(solution)/shard_map/step/pallas_call | solution.py:408
  69.4 1.3 %write_out.1 = (bf16[6,384,128]{2,1,0:T(8,128)(2,1)}, bf16[6,384,128]{2,1,0:T(8,128)(2,1)}, f32[6,80,128]{2,1,0:T(8,128)}, f32[6,80,128]{2,1,0:T(8,128)}, f32[6,80,128]{2,1,0:T(8,128)}) custom-call(bf16[6,384,128]{2,1,0:T(8,128)(2,1)S(1)} %get-tuple-element.15.refs_0_, bf16[6,384,128]{2,1,0:T(8,128)(2,1)S(1)} %get-tuple-element.16.refs_1_, ...), custom_call_target="tpu_custom_call" | custom-call | tf_op jit(solution)/shard_map/write_out/pallas_call | solution.py:438

commit v4 on v3

--- a/solution.py
+++ b/solution.py
@@ -203,11 +203,9 @@
     def mom(x_, i):
         return mb.at[x_ * 2 + core, i]
 
-    def mom_copies():
-        copies = []
-        for j, device in enumerate((*xn, across)):
-            copies += [copy(("mx", j, i), mom(x, i), mom(x, i), device) for i in range(2)]
-        return copies + [copy(("mc", 0, i), mom(x, i), mom(x, i), cn) for i in range(2)]
+    def mom_copies(i):
+        targets = [(("mx", j, i), device) for j, device in enumerate((*xn, across))]
+        return [copy(n, mom(x, i), mom(x, i), device) for n, device in (*targets, (("mc", 0, i), cn))]
 
     mom_y = [copy(("my", i), mom(x, i), mom(x, i), lows) for i in range(2)]
 
@@ -242,7 +240,7 @@
 
     @pl.when(lo == 0)
     def _():
-        for c in mom_copies():
+        for c in (*mom_copies(0), *mom_copies(1)):
             c.start()
 
     ag(3, 1, 2)
@@ -279,31 +277,39 @@
     rs(2, 0)
     rs(1, 1)
     rs(0, 2)
+    def mom_round(i):
+        @pl.when(lo == 1)
+        def _():
+            mom_y[i].wait_recv()
+            for c in mom_copies(i):
+                c.start()
+
     ag(6)
+    mom_round(0)
     rs(1, 2)
-    rs(3, 0)
-    ag(7)
+    mom_round(1)
+    ag(7, 0, 1)
     rs(2, 2)
     rs(2, 1)
-
-    @pl.when(lo == 1)
-    def _():
-        for c in mom_y:
-            c.wait_recv()
-        for c in mom_copies():
-            c.start()
 
     def hidden_grad(tokens, k, out):
         out[:, sub(k)] = jnp.dot(
             og_v[tokens, :], wb[:, sub(k)], preferred_element_type=F32
         ).astype(out.dtype)
 
-    for k in range(SUBS):
-        ag(8, k)
+    def hg_to(k):
         hidden_grad(theirs, k, hgs)
         send(("hg", k), hgs.at[:, sub(k)], hgr.at[:, sub(k)], far)
-    rs(3, 2)
-    rs(3, 1)
+
+    rs(3, 0)
+    ag(8, 0, 1)
+    for k in (2, 1):
+        rs(3, k)
+    hg_to(0)
+    hg_to(1)
+    ag(7, 2)
+    for k in (2, 1, 0):
+        rs(4, k)
     hidden_grad(own, 0, hg_own)
 
     same = (N_SLAB, N_SLAB)
@@ -325,8 +331,10 @@
             tuple(jnp.sum(jnp.where(here, v, 0)) for v in (old_own, old_rank, jnp.ones_like(old_own)))
         )
 
-    for k in range(SUBS):
-        rs(4, k)
+    ag(8, 2)
+    for k in (2, 1, 0):
+        rs(5, k)
+    hg_to(2)
     hidden_grad(own, 1, hg_own)
 
     def mom_on(j, x_):
@@ -334,9 +342,6 @@
             arrived(("mx", j, i), mom(x_, i), xn[0])
             send(("mc", j + 1, i), mom(x_, i), mom(x_, i), cn)
 
-    for k in range(SUBS):
-        rs(5, k)
-    hidden_grad(own, 2, hg_own)
     mom_on(0, x3)
     mom_on(1, x1)
 
@@ -353,11 +358,12 @@
                 dg_v[k, r, :] = (hg * fg[k, r, :]).astype(BF)
                 du_v[k, r, :] = (hg * fu[k, r, :]).astype(BF)
 
-    for k in range(SUBS):
+    for k in (2, 1, 0):
         rs(6, k)
+    hidden_grad(own, 2, hg_own)
     mom_on(2, x2)
     cotangents(0)
-    for k in range(SUBS):
+    for k in (2, 1, 0):
         rs(7, k)
     cotangents(1)
     cotangents(2)
@@ -376,7 +382,7 @@
         for i in range(2):
             ref = mb.at[x_ * 2 + 1 - core, i]
             arrived(("mc", j, i), ref, cn)
-    for k in range(SUBS):
+    for k in (2, 1, 0):
         rs(8, k)
         rs_sum(k)
         adam(k)
@@ -386,7 +392,7 @@
         for c in mom_y:
             c.wait_send()
 
-    for c in (*started.values(), *mom_copies()):
+    for c in (*started.values(), *mom_copies(0), *mom_copies(1)):
         c.wait_send()
 
 

time: 70.9 us -> 69.5 us (0.980); the launches traced: 70.7 us -> 68.6 us
  Pallas kernels: 70.1 us -> 68 us
    pallas_call x1, Pallas kernels: 68.8 us -> 66.7 us  [per_device(): pl.pallas_call(body, out_shape=[V(act, BF)] * 2 + [V(state, F32)] * 3, in...]
where the time goes in v4:
time: 69.5 us; the launch traced here: 68.6 us
  Pallas kernels  68 us (98%)
    pallas_call x1, Pallas kernels, per_device(): pl.pallas_call(body, out_shape=[V(act, BF)] * 2 + [V(state, F32)] * 3, in...  66.7 us

profile of v4, /device:TPU:24, one launch (start us, length us, event | category | flops | bytes accessed | tf_op | source)
XLA Modules:
  0.0 68.6 jit_solution(8617372553291100410)
XLA Ops:
  0.6 66.7 %step.1 = (bf16[6,384,128]{2,1,0:T(8,128)(2,1)S(1)}, bf16[6,384,128]{2,1,0:T(8,128)(2,1)S(1)}, f32[6,80,128]{2,1,0:T(8,128)S(1)}, f32[6,80,128]{2,1,0:T(8,128)S(1)}, f32[6,80,128]{2,1,0:T(8,128)S(1)}) custom-call(bf16[6,384,128]{2,1,0:T(8,128)(2,1)} %bitcast.32, bf16[6,384,128]{2,1,0:T(8,128)(2,1)} %bitcast.33, bf16[384,2560]{1,0:T(8,128)(2,1)} %og.1, ...), custom_call_target="tpu_custom_call" | custom-call | flops 6000000000 | bytes 12000000 | tf_op jit(solution)/shard_map/step/pallas_call | solution.py:414
  67.3 1.3 %write_out.1 = (bf16[6,384,128]{2,1,0:T(8,128)(2,1)}, bf16[6,384,128]{2,1,0:T(8,128)(2,1)}, f32[6,80,128]{2,1,0:T(8,128)}, f32[6,80,128]{2,1,0:T(8,128)}, f32[6,80,128]{2,1,0:T(8,128)}) custom-call(bf16[6,384,128]{2,1,0:T(8,128)(2,1)S(1)} %get-tuple-element.15.refs_0_, bf16[6,384,128]{2,1,0:T(8,128)(2,1)S(1)} %get-tuple-element.16.refs_1_, ...), custom_call_target="tpu_custom_call" | custom-call | tf_op jit(solution)/shard_map/write_out/pallas_call | solution.py:444

commit v5 on v4

--- a/solution.py
+++ b/solution.py
@@ -186,8 +186,13 @@
 
     own, theirs = pl.ds(0, TOK), pl.ds(TOK, TOK)
 
-    def hid_to(k):
-        send(("hid", k), hid.at[own, sub(k)], hid.at[theirs, sub(k)], far)
+    def hid_to(k, c):
+        name = ("hid", k)
+        started[SEND[name]] = copy(name, hid.at[own, sub(k)], hid.at[theirs, sub(k)], far)
+
+        @pl.when(core == c)
+        def _():
+            started[SEND[name]].start()
 
     def turn(tokens):
         for i in range(HALF // GB):
@@ -229,10 +234,13 @@
     for j, device in enumerate((*xn, across)):
         og_to(("ogx", j), x, device)
     og_to(("ogc", 0), x, cn)
-    hid_to(0)
+    hid_to(0, 0)
     ag(1, 1, 2)
+    hid_to(1, 0)
+    hid_to(0, 1)
     ag(2)
-    hid_to(1)
+    hid_to(2, 0)
+    hid_to(1, 1)
     ag(3, 0)
     for j, x_ in enumerate((x3, x1, x2)):
         arrived(("ogx", j), og_part(x_, core), xn[0])
@@ -244,7 +252,7 @@
             c.start()
 
     ag(3, 1, 2)
-    hid_to(2)
+    hid_to(2, 1)
     for j, x_ in enumerate((x, x3, x1, x2)):
         arrived(("ogc", j), og_part(x_, 1 - core), cn)
     turn(theirs)
@@ -306,11 +314,10 @@
     for k in (2, 1):
         rs(3, k)
     hg_to(0)
-    hg_to(1)
     ag(7, 2)
     for k in (2, 1, 0):
         rs(4, k)
-    hidden_grad(own, 0, hg_own)
+    hg_to(1)
 
     same = (N_SLAB, N_SLAB)
     lane, row = lax.broadcasted_iota(jnp.int32, same, 1), lax.broadcasted_iota(jnp.int32, same, 0)
@@ -335,7 +342,6 @@
     for k in (2, 1, 0):
         rs(5, k)
     hg_to(2)
-    hidden_grad(own, 1, hg_own)
 
     def mom_on(j, x_):
         for i in range(2):
@@ -360,13 +366,14 @@
 
     for k in (2, 1, 0):
         rs(6, k)
-    hidden_grad(own, 2, hg_own)
+    hidden_grad(own, 0, hg_own)
     mom_on(2, x2)
     cotangents(0)
     for k in (2, 1, 0):
         rs(7, k)
-    cotangents(1)
-    cotangents(2)
+    for k in (1, 2):
+        hidden_grad(own, k, hg_own)
+        cotangents(k)
     def adam(part):
         for k in range(part * CAP // SUBS, (part + 1) * CAP // SUBS):
             q, j, n = slots[k]

time: 69.5 us -> 69 us (level)
  no operation moved by 1% of the time
where the time goes in v5:
time: 69 us; the launch traced here: 68.6 us
  Pallas kernels  68 us (99%)
    pallas_call x1, Pallas kernels, per_device(): pl.pallas_call(body, out_shape=[V(act, BF)] * 2 + [V(state, F32)] * 3, in...  66.7 us

profile of v5, /device:TPU:24, one launch (start us, length us, event | category | flops | bytes accessed | tf_op | source)
XLA Modules:
  0.0 68.6 jit_solution(11314765191004742516)
XLA Ops:
  0.6 66.7 %step.1 = (bf16[6,384,128]{2,1,0:T(8,128)(2,1)S(1)}, bf16[6,384,128]{2,1,0:T(8,128)(2,1)S(1)}, f32[6,80,128]{2,1,0:T(8,128)S(1)}, f32[6,80,128]{2,1,0:T(8,128)S(1)}, f32[6,80,128]{2,1,0:T(8,128)S(1)}) custom-call(bf16[6,384,128]{2,1,0:T(8,128)(2,1)} %bitcast.32, bf16[6,384,128]{2,1,0:T(8,128)(2,1)} %bitcast.33, bf16[384,2560]{1,0:T(8,128)(2,1)} %og.1, ...), custom_call_target="tpu_custom_call" | custom-call | flops 6000000000 | bytes 12000000 | tf_op jit(solution)/shard_map/step/pallas_call | solution.py:421
  67.3 1.3 %write_out.1 = (bf16[6,384,128]{2,1,0:T(8,128)(2,1)}, bf16[6,384,128]{2,1,0:T(8,128)(2,1)}, f32[6,80,128]{2,1,0:T(8,128)}, f32[6,80,128]{2,1,0:T(8,128)}, f32[6,80,128]{2,1,0:T(8,128)}) custom-call(bf16[6,384,128]{2,1,0:T(8,128)(2,1)S(1)} %get-tuple-element.15.refs_0_, bf16[6,384,128]{2,1,0:T(8,128)(2,1)S(1)} %get-tuple-element.16.refs_1_, ...), custom_call_target="tpu_custom_call" | custom-call | tf_op jit(solution)/shard_map/write_out/pallas_call | solution.py:451

commit v6 on v5

--- a/solution.py
+++ b/solution.py
@@ -280,11 +280,11 @@
     rs(1, 0)
     rs(0, 1)
     mom_y_start(1)
+    gradient(2)
+    rs(0, 2)
     ag(5)
-    gradient(2)
     rs(2, 0)
     rs(1, 1)
-    rs(0, 2)
     def mom_round(i):
         @pl.when(lo == 1)
         def _():

time: 69 us -> 69.7 us (1.010)
  the two profiles are of different devices: /device:TPU:24 before, /device:TPU:16 now
where the time goes in v6:
time: 69.7 us; the launch traced here: 69.6 us
  Pallas kernels  69 us (99%)
    pallas_call x1, Pallas kernels, per_device(): pl.pallas_call(body, out_shape=[V(act, BF)] * 2 + [V(state, F32)] * 3, in...  67.7 us

profile of v6, /device:TPU:16, one launch (start us, length us, event | category | flops | bytes accessed | tf_op | source)
XLA Modules:
  0.0 69.6 jit_solution(869646947650153171)
XLA Ops:
  0.6 67.7 %step.1 = (bf16[6,384,128]{2,1,0:T(8,128)(2,1)S(1)}, bf16[6,384,128]{2,1,0:T(8,128)(2,1)S(1)}, f32[6,80,128]{2,1,0:T(8,128)S(1)}, f32[6,80,128]{2,1,0:T(8,128)S(1)}, f32[6,80,128]{2,1,0:T(8,128)S(1)}) custom-call(bf16[6,384,128]{2,1,0:T(8,128)(2,1)} %bitcast.32, bf16[6,384,128]{2,1,0:T(8,128)(2,1)} %bitcast.33, bf16[384,2560]{1,0:T(8,128)(2,1)} %og.1, ...), custom_call_target="tpu_custom_call" | custom-call | flops 6000000000 | bytes 12000000 | tf_op jit(solution)/shard_map/step/pallas_call | solution.py:421
  68.3 1.3 %write_out.1 = (bf16[6,384,128]{2,1,0:T(8,128)(2,1)}, bf16[6,384,128]{2,1,0:T(8,128)(2,1)}, f32[6,80,128]{2,1,0:T(8,128)}, f32[6,80,128]{2,1,0:T(8,128)}, f32[6,80,128]{2,1,0:T(8,128)}) custom-call(bf16[6,384,128]{2,1,0:T(8,128)(2,1)S(1)} %get-tuple-element.15.refs_0_, bf16[6,384,128]{2,1,0:T(8,128)(2,1)S(1)} %get-tuple-element.16.refs_1_, ...), custom_call_target="tpu_custom_call" | custom-call | tf_op jit(solution)/shard_map/write_out/pallas_call | solution.py:451
